TPU v7x, 32 devices: a whole 2x2x4 slice. The times are simulated.
32 devices in a mesh: fsdp: 8 (over y, x, core), seq: 4 (over z).
Axes of the slice: x: 2, y: 2, z: 4, core: 2. Of those that a mesh axis runs over, the one named last changes fastest.
Arguments:
- block_in: bfloat16 [20480, 640], P(('fsdp', 'seq')), may hold values from -134 to 134
- query_weight: bfloat16 [640, 1024], P('fsdp'), may hold values from -0.25 to 0.25
- key_weight: bfloat16 [640, 256], P('fsdp'), may hold values from -0.25 to 0.25
- value_weight: bfloat16 [640, 256], P('fsdp'), may hold values from -0.25 to 0.25
- output_weight: bfloat16 [1024, 640], P('fsdp'), may hold values from -0.1875 to 0.1875
- gate_weight: bfloat16 [640, 2048], P('fsdp'), may hold values from -0.25 to 0.25
- up_weight: bfloat16 [640, 2048], P('fsdp'), may hold values from -0.25 to 0.25
- down_weight: bfloat16 [2048, 640], P('fsdp'), may hold values from -0.125 to 0.125
- attention_norm: bfloat16 [640], P('fsdp'), may hold values from 0.099609375 to 1.8984375
- query_norm: bfloat16 [256], P('fsdp'), may hold values from 0.099609375 to 1.8984375
- key_norm: bfloat16 [256], P('fsdp'), may hold values from 0.099609375 to 1.8984375
- post_attention_norm: bfloat16 [640], P('fsdp'), may hold values from 0.099609375 to 1.8984375
- feedforward_norm: bfloat16 [640], P('fsdp'), may hold values from 0.099609375 to 1.8984375
- post_feedforward_norm: bfloat16 [640], P('fsdp'), may hold values from 0.099609375 to 1.8984375
- grad_out: bfloat16 [20480, 640], P(('fsdp', 'seq')), may hold values from -6 to 6
Outputs:
- block_out: bfloat16 [20480, 640], P(('fsdp', 'seq'))
- grad_in: bfloat16 [20480, 640], P(('fsdp', 'seq'))
- grad_query_weight: float32 [640, 1024], P('fsdp')
- grad_key_weight: float32 [640, 256], P('fsdp')
- grad_value_weight: float32 [640, 256], P('fsdp')
- grad_output_weight: float32 [1024, 640], P('fsdp')
- grad_gate_weight: float32 [640, 2048], P('fsdp')
- grad_up_weight: float32 [640, 2048], P('fsdp')
- grad_down_weight: float32 [2048, 640], P('fsdp')
- grad_attention_norm: float32 [640], P('fsdp')
- grad_query_norm: float32 [256], P('fsdp')
- grad_key_norm: float32 [256], P('fsdp')
- grad_post_attention_norm: float32 [640], P('fsdp')
- grad_feedforward_norm: float32 [640], P('fsdp')
- grad_post_feedforward_norm: float32 [640], P('fsdp')
All inputs are finite; a program needn't handle non-finite values.
Results may differ from a plain program's by a relative error of at most 0.018.
Values may be sent and summed in bfloat16 or wider, within the bound.
A program may use at most 128 MiB of HBM per device.

v0:
```python
import jax
import jax.numpy as jnp
from jax import lax
from jax.sharding import PartitionSpec as P

epsilon = 1e-06
rope_base = 1000000.0
negative = -1e30


def rms_scale(values, gain_row):
    return values * lax.rsqrt(jnp.mean(values * values, -1, keepdims=True) + epsilon) * gain_row


def rotate(values, cosine_table, sine_table):
    half_width = values.shape[-1] // 2
    first_half = values[..., :half_width]
    second = values[..., half_width:]
    return jnp.concatenate(
        [
            first_half * cosine_table - second * sine_table,
            second * cosine_table + first_half * sine_table,
        ],
        -1,
    )


def angles_for(positions, width):
    half_width = width // 2
    frequency = rope_base ** (-(jnp.arange(half_width).astype(jnp.float32) * 2.0 / width))
    angles = positions[:, None] * frequency[None, :]
    return (jnp.cos(angles), jnp.sin(angles))


def gelu_product(gate_lin, up_lin):
    return jax.nn.gelu(gate_lin, approximate=True) * up_lin


def rounded(values):
    return lax.optimization_barrier(values.astype(jnp.bfloat16)).astype(jnp.float32)


def masked_scores(query_rows, key_rows, first_pos, score_scale):
    block_rows = query_rows.shape[0]
    scores = (
        jnp.einsum("qhd,kd->hqk", query_rows, key_rows, preferred_element_type=jnp.float32)
        * score_scale
    )
    query_pos = first_pos + jnp.arange(block_rows, dtype=jnp.int32)
    key_pos = jnp.arange(key_rows.shape[0], dtype=jnp.int32)
    allowed = key_pos[None, :] <= query_pos[:, None]
    return jnp.where(allowed[None], scores, negative)


def attend_forward(queries, key_rows, value_rows, block_rows, query_offset):
    score_scale = queries.shape[-1] ** (-0.5)

    def one_block(block_index):
        row_start = block_index * block_rows
        query_rows = lax.dynamic_slice_in_dim(queries, row_start, block_rows, 0)
        scores = masked_scores(query_rows, key_rows, query_offset + row_start, score_scale)
        row_max = jnp.max(scores, -1, keepdims=True)
        exp_scores = jnp.exp(scores - row_max)
        row_total = jnp.sum(exp_scores, -1, keepdims=True)
        weights_low = (exp_scores / row_total).astype(jnp.bfloat16)
        block_out = jnp.einsum(
            "hqk,kd->qhd", weights_low, value_rows, preferred_element_type=jnp.float32
        )
        return (block_out, (row_max + jnp.log(row_total))[..., 0])

    outputs, log_totals = lax.map(
        one_block, jnp.arange(queries.shape[0] // block_rows, dtype=jnp.int32)
    )
    return (outputs.reshape(queries.shape), log_totals)


def attend_backward(queries, key_rows, value_rows, grad_rows, log_totals, block_rows, query_offset):
    score_scale = queries.shape[-1] ** (-0.5)

    def one_block(running, block_index):
        key_grad, value_grad = running
        row_start = block_index * block_rows
        query_rows = lax.dynamic_slice_in_dim(queries, row_start, block_rows, 0)
        grad_block = lax.dynamic_slice_in_dim(grad_rows, row_start, block_rows, 0)
        scores = masked_scores(query_rows, key_rows, query_offset + row_start, score_scale)
        weights = jnp.exp(scores - log_totals[block_index][..., None])
        grad_weights = jnp.einsum(
            "qhd,kd->hqk", grad_block, value_rows, preferred_element_type=jnp.float32
        )
        inner = jnp.sum(weights * grad_weights, -1, keepdims=True)
        grad_scores = (weights * (grad_weights - inner)).astype(jnp.bfloat16)
        query_grad = (
            jnp.einsum("hqk,kd->qhd", grad_scores, key_rows, preferred_element_type=jnp.float32)
            * score_scale
        )
        key_grad = (
            key_grad
            + jnp.einsum("hqk,qhd->kd", grad_scores, query_rows, preferred_element_type=jnp.float32)
            * score_scale
        )
        value_grad = value_grad + jnp.einsum(
            "hqk,qhd->kd",
            weights.astype(jnp.bfloat16),
            grad_block,
            preferred_element_type=jnp.float32,
        )
        return ((key_grad, value_grad), query_grad)

    zeros_rows = jnp.zeros(key_rows.shape, jnp.float32)
    (key_grad, value_grad), query_grads = lax.scan(
        one_block,
        (zeros_rows, zeros_rows),
        jnp.arange(queries.shape[0] // block_rows, dtype=jnp.int32),
    )
    return (query_grads.reshape(queries.shape), key_grad, value_grad)


def per_device(
    block_in,
    query_weight,
    key_weight,
    value_weight,
    output_weight,
    gate_weight,
    up_weight,
    down_weight,
    attention_norm,
    query_norm,
    key_norm,
    post_attention_norm,
    feedforward_norm,
    post_feedforward_norm,
    grad_out,
):
    gathered = (
        lax.all_gather(query_weight, "fsdp", axis=0, tiled=True),
        lax.all_gather(key_weight, "fsdp", axis=0, tiled=True),
        lax.all_gather(value_weight, "fsdp", axis=0, tiled=True),
        lax.all_gather(output_weight, "fsdp", axis=0, tiled=True),
        lax.all_gather(gate_weight, "fsdp", axis=0, tiled=True),
        lax.all_gather(up_weight, "fsdp", axis=0, tiled=True),
        lax.all_gather(down_weight, "fsdp", axis=0, tiled=True),
        lax.all_gather(attention_norm, "fsdp", axis=0, tiled=True),
        lax.all_gather(query_norm, "fsdp", axis=0, tiled=True),
        lax.all_gather(key_norm, "fsdp", axis=0, tiled=True),
        lax.all_gather(post_attention_norm, "fsdp", axis=0, tiled=True),
        lax.all_gather(feedforward_norm, "fsdp", axis=0, tiled=True),
        lax.all_gather(post_feedforward_norm, "fsdp", axis=0, tiled=True),
    )
    query_full, key_full, value_full, output_full, gate_full, up_full, down_full = gathered[:7]
    norm_gains = tuple((gain_row.astype(jnp.float32) for gain_row in gathered[7:]))
    attention_gain, query_gain, key_gain, post_attention_gain, second_gain, post_second_gain = (
        norm_gains
    )
    token_count = block_in.shape[0]
    head_size = query_gain.shape[0]
    head_count = query_full.shape[1] // head_size
    length = token_count * lax.axis_size("seq")
    block_rows = min(512, length)
    token_offset = lax.axis_index("seq") * token_count
    input_f = block_in.astype(jnp.float32)
    normed, pull_normed = jax.vjp(rms_scale, input_f, attention_gain)
    normed_low = normed.astype(jnp.bfloat16)
    query_lin = jnp.dot(normed_low, query_full, preferred_element_type=jnp.float32).reshape(
        token_count, head_count, head_size
    )
    key_lin = jnp.dot(normed_low, key_full, preferred_element_type=jnp.float32)
    value_low = jnp.dot(normed_low, value_full, preferred_element_type=jnp.float32).astype(
        jnp.bfloat16
    )
    positions = (token_offset + jnp.arange(token_count, dtype=jnp.int32)).astype(jnp.float32)
    cosine_table, sine_table = angles_for(positions, head_size)

    def query_piece(values, gain_row):
        return rotate(rms_scale(values, gain_row), cosine_table[:, None, :], sine_table[:, None, :])

    def key_piece(values, gain_row):
        return rotate(rms_scale(values, gain_row), cosine_table, sine_table)

    queries, pull_queries = jax.vjp(query_piece, query_lin, query_gain)
    key_rows, pull_keys = jax.vjp(key_piece, key_lin, key_gain)
    queries_low = queries.astype(jnp.bfloat16)
    key_all, value_all = (
        lax.all_gather(key_rows.astype(jnp.bfloat16), "seq", axis=0, tiled=True),
        lax.all_gather(value_low, "seq", axis=0, tiled=True),
    )
    query_heads = lax.all_to_all(queries_low, "seq", split_axis=1, concat_axis=0, tiled=True)
    head_out, log_totals = attend_forward(query_heads, key_all, value_all, block_rows, 0)
    mixed = lax.all_to_all(
        head_out.astype(jnp.bfloat16), "seq", split_axis=0, concat_axis=1, tiled=True
    ).reshape(token_count, head_count * head_size)
    attended = jnp.dot(mixed, output_full, preferred_element_type=jnp.float32)
    post_branch, pull_post = jax.vjp(rms_scale, attended, post_attention_gain)
    residual = input_f + post_branch
    normed_second, pull_second = jax.vjp(rms_scale, residual, second_gain)
    second_low = normed_second.astype(jnp.bfloat16)
    gate_lin = jnp.dot(second_low, gate_full, preferred_element_type=jnp.float32)
    up_lin = jnp.dot(second_low, up_full, preferred_element_type=jnp.float32)
    activated, pull_activated = jax.vjp(gelu_product, gate_lin, up_lin)
    activated_low = activated.astype(jnp.bfloat16)
    down_lin = jnp.dot(activated_low, down_full, preferred_element_type=jnp.float32)
    tail_branch, pull_tail = jax.vjp(rms_scale, down_lin, post_second_gain)
    block_out = (residual + tail_branch).astype(jnp.bfloat16)
    weights_back = (
        lax.all_gather(query_weight, "fsdp", axis=0, tiled=True),
        lax.all_gather(key_weight, "fsdp", axis=0, tiled=True),
        lax.all_gather(value_weight, "fsdp", axis=0, tiled=True),
        lax.all_gather(output_weight, "fsdp", axis=0, tiled=True),
        lax.all_gather(gate_weight, "fsdp", axis=0, tiled=True),
        lax.all_gather(up_weight, "fsdp", axis=0, tiled=True),
        lax.all_gather(down_weight, "fsdp", axis=0, tiled=True),
    )
    query_back, key_back, value_back, output_back, gate_back, up_back, down_back = weights_back
    grad_f = grad_out.astype(jnp.float32)
    grad_down, grad_post_second = pull_tail(grad_f)
    grad_down_low = grad_down.astype(jnp.bfloat16)
    grad_down_weight = jnp.einsum(
        "tf,td->fd", activated_low, grad_down_low, preferred_element_type=jnp.float32
    )
    grad_activated = jnp.einsum(
        "td,fd->tf", grad_down_low, down_back, preferred_element_type=jnp.float32
    )
    grad_gate, grad_up = pull_activated(grad_activated)
    gate_low = grad_gate.astype(jnp.bfloat16)
    up_low = grad_up.astype(jnp.bfloat16)
    grad_gate_weight = jnp.einsum(
        "td,tf->df", second_low, gate_low, preferred_element_type=jnp.float32
    )
    grad_up_weight = jnp.einsum("td,tf->df", second_low, up_low, preferred_element_type=jnp.float32)
    grad_second = jnp.einsum(
        "tf,df->td", gate_low, gate_back, preferred_element_type=jnp.float32
    ) + jnp.einsum("tf,df->td", up_low, up_back, preferred_element_type=jnp.float32)
    grad_resid_part, grad_second_gain = pull_second(grad_second)
    grad_residual = grad_f + grad_resid_part
    grad_attended, grad_post_attention = pull_post(grad_residual)
    attended_low = grad_attended.astype(jnp.bfloat16)
    grad_output_weight = jnp.einsum(
        "tq,td->qd", mixed, attended_low, preferred_element_type=jnp.float32
    )
    grad_mixed = (
        jnp.einsum("td,qd->tq", attended_low, output_back, preferred_element_type=jnp.float32)
        .astype(jnp.bfloat16)
        .reshape(token_count, head_count, head_size)
    )
    grad_head_rows = lax.all_to_all(grad_mixed, "seq", split_axis=1, concat_axis=0, tiled=True)
    query_head_grad, key_all_grad, value_all_grad = attend_backward(
        query_heads, key_all, value_all, grad_head_rows, log_totals, block_rows, 0
    )
    grad_queries = lax.all_to_all(
        query_head_grad.astype(jnp.bfloat16), "seq", split_axis=0, concat_axis=1, tiled=True
    )
    grad_keys, grad_values = (
        lax.psum_scatter(
            key_all_grad.astype(jnp.bfloat16), "seq", scatter_dimension=0, tiled=True
        ).astype(jnp.float32),
        lax.psum_scatter(
            value_all_grad.astype(jnp.bfloat16), "seq", scatter_dimension=0, tiled=True
        ).astype(jnp.float32),
    )
    grad_query_lin, grad_query_gain = pull_queries(grad_queries.astype(jnp.float32))
    grad_key_lin, grad_key_gain = pull_keys(rounded(grad_keys))
    query_lin_low = grad_query_lin.reshape(token_count, head_count * head_size).astype(jnp.bfloat16)
    key_lin_low = grad_key_lin.astype(jnp.bfloat16)
    value_lin_low = grad_values.astype(jnp.bfloat16)
    grad_query_weight = jnp.einsum(
        "td,tq->dq", normed_low, query_lin_low, preferred_element_type=jnp.float32
    )
    grad_key_weight = jnp.einsum(
        "td,tq->dq", normed_low, key_lin_low, preferred_element_type=jnp.float32
    )
    grad_value_weight = jnp.einsum(
        "td,tq->dq", normed_low, value_lin_low, preferred_element_type=jnp.float32
    )
    grad_normed = jnp.einsum(
        "tq,dq->td", query_lin_low, query_back, preferred_element_type=jnp.float32
    )
    grad_normed = grad_normed + jnp.einsum(
        "tq,dq->td", key_lin_low, key_back, preferred_element_type=jnp.float32
    )
    grad_normed = grad_normed + jnp.einsum(
        "tq,dq->td", value_lin_low, value_back, preferred_element_type=jnp.float32
    )
    grad_input_part, grad_attention_gain = pull_normed(grad_normed)
    grad_in = (grad_residual + grad_input_part).astype(jnp.bfloat16)
    scattered = (
        lax.psum_scatter(grad_query_weight, "fsdp", scatter_dimension=0, tiled=True),
        lax.psum_scatter(grad_key_weight, "fsdp", scatter_dimension=0, tiled=True),
        lax.psum_scatter(grad_value_weight, "fsdp", scatter_dimension=0, tiled=True),
        lax.psum_scatter(grad_output_weight, "fsdp", scatter_dimension=0, tiled=True),
        lax.psum_scatter(grad_gate_weight, "fsdp", scatter_dimension=0, tiled=True),
        lax.psum_scatter(grad_up_weight, "fsdp", scatter_dimension=0, tiled=True),
        lax.psum_scatter(grad_down_weight, "fsdp", scatter_dimension=0, tiled=True),
        lax.psum_scatter(grad_attention_gain, "fsdp", scatter_dimension=0, tiled=True),
        lax.psum_scatter(grad_query_gain, "fsdp", scatter_dimension=0, tiled=True),
        lax.psum_scatter(grad_key_gain, "fsdp", scatter_dimension=0, tiled=True),
        lax.psum_scatter(grad_post_attention, "fsdp", scatter_dimension=0, tiled=True),
        lax.psum_scatter(grad_second_gain, "fsdp", scatter_dimension=0, tiled=True),
        lax.psum_scatter(grad_post_second, "fsdp", scatter_dimension=0, tiled=True),
    )
    summed = (
        lax.psum(scattered[0].astype(jnp.bfloat16), "seq").astype(jnp.float32),
        lax.psum(scattered[1].astype(jnp.bfloat16), "seq").astype(jnp.float32),
        lax.psum(scattered[2].astype(jnp.bfloat16), "seq").astype(jnp.float32),
        lax.psum(scattered[3].astype(jnp.bfloat16), "seq").astype(jnp.float32),
        lax.psum(scattered[4].astype(jnp.bfloat16), "seq").astype(jnp.float32),
        lax.psum(scattered[5].astype(jnp.bfloat16), "seq").astype(jnp.float32),
        lax.psum(scattered[6].astype(jnp.bfloat16), "seq").astype(jnp.float32),
        lax.psum(scattered[7].astype(jnp.bfloat16), "seq").astype(jnp.float32),
        lax.psum(scattered[8].astype(jnp.bfloat16), "seq").astype(jnp.float32),
        lax.psum(scattered[9].astype(jnp.bfloat16), "seq").astype(jnp.float32),
        lax.psum(scattered[10].astype(jnp.bfloat16), "seq").astype(jnp.float32),
        lax.psum(scattered[11].astype(jnp.bfloat16), "seq").astype(jnp.float32),
        lax.psum(scattered[12].astype(jnp.bfloat16), "seq").astype(jnp.float32),
    )
    return (
        block_out,
        grad_in,
        summed[0],
        summed[1],
        summed[2],
        summed[3],
        summed[4],
        summed[5],
        summed[6],
        summed[7],
        summed[8],
        summed[9],
        summed[10],
        summed[11],
        summed[12],
    )


def solution(mesh):
    in_specs = (
        P(("fsdp", "seq"), None),
        P("fsdp", None),
        P("fsdp", None),
        P("fsdp", None),
        P("fsdp", None),
        P("fsdp", None),
        P("fsdp", None),
        P("fsdp", None),
        P("fsdp"),
        P("fsdp"),
        P("fsdp"),
        P("fsdp"),
        P("fsdp"),
        P("fsdp"),
        P(("fsdp", "seq"), None),
    )
    out_specs = (
        P(("fsdp", "seq"), None),
        P(("fsdp", "seq"), None),
        P("fsdp", None),
        P("fsdp", None),
        P("fsdp", None),
        P("fsdp", None),
        P("fsdp", None),
        P("fsdp", None),
        P("fsdp", None),
        P("fsdp"),
        P("fsdp"),
        P("fsdp"),
        P("fsdp"),
        P("fsdp"),
        P("fsdp"),
    )
    return jax.shard_map(
        per_device, mesh=mesh, in_specs=in_specs, out_specs=out_specs, check_vma=False
    )
```

profile of v0, /device:TPU:0, one launch (start us, length us, event | category | flops | bytes accessed | tf_op | source)
XLA Modules:
  0.0 985.4 jit_solution(9208684761553230560)
XLA Ops:
  14.0 15.8 %all-reduce.17 = (bf16[640]{0:T(1024)(128)(2,1)S(1)}, bf16[256]{0:T(256)(128)(2,1)S(1)}, bf16[256]{0:T(256)(128)(2,1)S(1)}, bf16[640]{0:T(1024)(128)(2,1)S(1)}, ...) all-reduce(bf16[640]{0:T(1024)(128)(2,1)S(1)} %dynamic-update-slice, ...), channel_id=1, replica_groups=mesh['fsdp'=8,'seq'=4] {'fsdp'}, use_global_device_ids=true, to_apply=%add.4 | all-reduce | flops 3072 | bytes 12288
  29.8 8.8 all_gather.55
  43.4 9.5 all_gather.58
  78.5 49.1 %all-gather.12.cloned.1.call-done = bf16[2560,256]{1,0:T(8,128)(2,1)} async-done(((bf16[640,256]{1,0:T(8,128)(2,1)}), bf16[2560,256]{1,0:T(8,128)(2,1)}) %all-gather.12.cloned.1.call-update) | async-done | bytes 1310736 | tf_op jit(solution)/shard_map/all_gather | solution.py:185
  128.5 35.3 %while.27 = (s32[]{:T(128)}, bf16[5,512,1,256]{3,1,2,0:T(8,128)(2,1)S(1)}, f32[5,1,512]{2,1,0:T(1,128)S(1)}, s32[5]{0:T(128)S(1)}, bf16[2560,1,256]{2,0,1:T(8,12...) while((s32[]{:T(128)}, ...), condition=%wide.region_6.7_spmd, body=%wide.region_3.6_spmd.sunk | while | flops 1353973760 | bytes 19161280 | solution.py:71
  173.9 28.6 %all-to-all-done.1 = bf16[4,2,81920]{2,1,0:T(2,128)(2,1)S(1)} async-done(((bf16[4,2,81920]{2,1,0:T(2,128)(2,1)}), bf16[4,2,81920]{2,1,0:T(2,128)(2,1)S(1)}, u32[]{:S(2)}, u32[]{:S(2)}) %all-to-all-start.1) | async-done | bytes 1310752 | tf_op jit(solution)/shard_map/all_to_all | solution.py:189
  214.0 6.6 fusion.94
  220.6 10.1 %multiply_convert_fusion.1 = (bf16[640,2048]{1,0:T(8,128)(2,1)}, f32[640,2048]{1,0:T(8,128)}) fusion(f32[640,2048]{1,0:T(8,128)} %fusion.94, bf16[640,640]{0,1:T(8,128)(2,1)} %multiply_convert_fusion.2, bf16[640,2048]{1,0:T(8,128)(2,1)} %all-gather.18.cloned.1.call-done), kind=kOutput, calls=%fused_computation.58 | convolution fusion | flops 1690828800 | bytes 16547840 | tf_op jit(solution)/shard_map/dot_general | solution.py:198
  230.7 18.3 %all-gather.20.cloned.1.call-done = bf16[2048,640]{1,0:T(8,128)(2,1)} async-done(((bf16[256,640]{1,0:T(8,128)(2,1)}), bf16[2048,640]{1,0:T(8,128)(2,1)}) %all-gather.20.cloned.1.call-update) | async-done | bytes 2621456 | tf_op jit(solution)/shard_map/all_gather | solution.py:142
  258.6 6.7 multiply_convert_fusion
  281.4 31.9 %all-to-all-done.2 = bf16[640,4,256]{2,0,1:T(8,128)(2,1)} async-done(((bf16[640,4,256]{2,0,1:T(8,128)(2,1)}), bf16[640,4,256]{2,0,1:T(8,128)(2,1)}, u32[]{:S(2)}, u32[]{:S(2)}) %all-to-all-start.2) | async-done | bytes 1310752 | tf_op jit(solution)/shard_map/all_to_all | solution.py:245
  314.4 135.8 %while.28 = (s32[]{:T(128)}, f32[2560,256]{1,0:T(8,128)}, f32[2560,256]{1,0:T(8,128)}, bf16[5,512,1,256]{3,1,2,0:T(8,128)(2,1)}, s32[5]{0:T(128)S(1)}, /*index=5...) while((s32[]{:T(128)}, f32[2560,256]{1,0:T(8,128)}, ...), condition=%wide.region_15.16_spmd.clone, body=%wide.region_13.15_spmd.clone.sunk | while | flops 3371958272 | bytes 133970368 | solution.py:110
  457.0 28.1 %reduce-scatter.28.cloned.1.call-done = bf16[640,256]{1,0:T(8,128)(2,1)} async-done(((bf16[2560,256]{1,0:T(8,128)(2,1)}), bf16[640,256]{1,0:T(8,128)(2,1)}) %reduce-scatter.28.cloned.1.call-update) | async-done | bytes 327696
  490.4 27.1 %reduce-scatter.12.cloned.1.call-done = bf16[640,256]{1,0:T(8,128)(2,1)} async-done(((bf16[2560,256]{1,0:T(8,128)(2,1)}), bf16[640,256]{1,0:T(8,128)(2,1)}) %reduce-scatter.12.cloned.1.call-update) | async-done | bytes 327696 | tf_op jit(solution)/shard_map/reduce_scatter | solution.py:256
  526.1 34.8 %all_to_all.60 = bf16[4,2,81920]{2,1,0:T(2,128)(2,1)} all-to-all(bf16[4,2,81920]{2,1,0:T(2,128)(2,1)S(1)} %reshape.445), channel_id=1, replica_groups=mesh['fsdp'=8,'seq'=4] {'seq'}, dimensions={0} | all-to-all | bytes 2621440 | tf_op jit(solution)/shard_map/all_to_all | solution.py:249
  587.4 6.6 fusion.100
  599.8 23.3 %all-reduce.16 = (bf16[640]{0:T(1024)(128)(2,1)S(1)}, bf16[256]{0:T(256)(128)(2,1)S(1)}, bf16[256]{0:T(256)(128)(2,1)S(1)}, bf16[640]{0:T(1024)(128)(2,1)S(1)}, ...) all-reduce(f32[640]{0:T(1024)S(1)} %get-tuple-element.377, ...), channel_id=11, replica_groups=mesh['fsdp'=8,'seq'=4] {'fsdp'}, use_global_device_ids=true, to_apply=%region_36.37.clone | all-reduce | flops 3072 | bytes 18432
  629.7 9.9 %reduce-scatter.20.cloned.1.call-done = f32[128,640]{1,0:T(8,128)} async-done(((f32[1024,640]{1,0:T(8,128)}), f32[128,640]{1,0:T(8,128)}) %reduce-scatter.20.cloned.1.call-update) | async-done | bytes 327696 | tf_op jit(solution)/shard_map/reduce_scatter | solution.py:289
  641.3 45.4 %reduce-scatter.14.cloned.1.call-done = f32[80,1024]{1,0:T(8,128)} async-done(((f32[640,1024]{1,0:T(8,128)}), f32[80,1024]{1,0:T(8,128)}) %reduce-scatter.14.cloned.1.call-update) | async-done | bytes 327696 | tf_op jit(solution)/shard_map/reduce_scatter | solution.py:286
  688.3 58.2 %reduce-scatter.22.cloned.1.call-done = f32[80,2048]{1,0:T(8,128)} async-done(((f32[640,2048]{1,0:T(8,128)}), f32[80,2048]{1,0:T(8,128)}) %reduce-scatter.22.cloned.1.call-update) | async-done | bytes 655376 | tf_op jit(solution)/shard_map/reduce_scatter | solution.py:290
  748.3 58.3 %reduce-scatter.24.cloned.1.call-done = f32[80,2048]{1,0:T(8,128)} async-done(((f32[640,2048]{1,0:T(8,128)}), f32[80,2048]{1,0:T(8,128)}) %reduce-scatter.24.cloned.1.call-update) | async-done | bytes 655376 | tf_op jit(solution)/shard_map/reduce_scatter | solution.py:291
  808.5 58.0 %reduce-scatter.26.cloned.1.call-done = f32[256,640]{1,0:T(8,128)} async-done(((f32[2048,640]{1,0:T(8,128)}), f32[256,640]{1,0:T(8,128)}) %reduce-scatter.26.cloned.1.call-update) | async-done | bytes 655376 | tf_op jit(solution)/shard_map/reduce_scatter | solution.py:292
  873.2 32.1 %all-reduce.23.cloned.1.call-done = (bf16[80,256]{1,0:T(8,128)(2,1)}, bf16[80,256]{1,0:T(8,128)(2,1)}, bf16[80]{0:T(256)(128)(2,1)}, bf16[32]{0:T(256)(128)(2,1)...) async-done(((bf16[80,256]{1,0:T(8,128)(2,1)}, bf16[80,256]{1,0:T(8,128)(2,1)}, bf16[80]{0:T(256)(128)(2,1)}, ...) | async-done | bytes 82704 | tf_op jit(solution)/shard_map/psum | solution.py:302
  915.0 56.3 %all-reduce.25.cloned.1.call-done = (bf16[80,1024]{1,0:T(8,128)(2,1)}, bf16[128,640]{1,0:T(8,128)(2,1)}, bf16[80,2048]{1,0:T(8,128)(2,1)}, bf16[80,2048]{1,0:T(8,128)(2,1)}, bf16[256,640]{1,0:T(8,128)(2,1)}) async-done(((bf16[80,1024]{1,0:T(8,128)(2,1)}, bf16[128,640]{1,0:T(8,128)(2,1)}, bf16[80,2048]{1,0:T(8,128)(2,1)}, bf16[80,2048]{1,0:T(8,128)(2,1)}, bf16[256,640]{1,0:T(8,128)(2,1)}), ...) | async-done | bytes 1310736 | tf_op jit(solution)/shard_map/psum | solution.py:301
  (463 shorter events, 326.5 us)
Async XLA Ops:
  7.3 50.7 %all-gather.8.cloned.1.call-start = ((), (), s32[]{:S(2)}) async-start(), calls=%async_computation.13 | async-start | bytes 1474560 | tf_op jit(solution)/shard_map/all_gather | solution.py:136
  8.0 68.0 %all-gather.10.cloned.1.call-start = ((), (), s32[]{:S(2)}) async-start(), calls=%async_computation.14 | async-start | bytes 1638400 | tf_op jit(solution)/shard_map/all_gather | solution.py:184
  43.3 84.3 %all-gather.12.cloned.1.call-start = ((), (), s32[]{:S(2)}) async-start(), calls=%async_computation.15 | async-start | bytes 1638400 | tf_op jit(solution)/shard_map/all_gather | solution.py:185
  54.9 153.8 %all-gather.14.cloned.1.call-start = ((), (), s32[]{:S(2)}) async-start(), calls=%async_computation.16 | async-start | bytes 1474560 | tf_op jit(solution)/shard_map/all_gather | solution.py:139
  55.5 158.5 %all-gather.16.cloned.1.call-start = ((), (), s32[]{:S(2)}) async-start(), calls=%async_computation.17 | async-start | bytes 2949120 | tf_op jit(solution)/shard_map/all_gather | solution.py:140
  70.6 57.8 %all-to-all-start = ((bf16[640,4,256]{2,0,1:T(8,128)(2,1)}), bf16[640,4,256]{2,0,1:T(8,128)(2,1)}, u32[]{:S(2)}, u32[]{:S(2)}) async-start(bf16[640,4,256]{2,0,1:T(8,128)(2,1)} %pad_maximum_fusion), calls=%async_computation | async-start | bytes 2621440 | tf_op jit(solution)/shard_map/all_to_all | solution.py:187
  75.4 145.2 %all-gather.18.cloned.1.call-start = ((), (), s32[]{:S(2)}) async-start(), calls=%async_computation.18 | async-start | bytes 2949120 | tf_op jit(solution)/shard_map/all_gather | solution.py:141
  167.7 34.8 %all-to-all-start.1 = ((bf16[4,2,81920]{2,1,0:T(2,128)(2,1)}), bf16[4,2,81920]{2,1,0:T(2,128)(2,1)S(1)}, u32[]{:S(2)}, u32[]{:S(2)}) async-start(bf16[4,2,81920]{2,1,0:T(2,128)(2,1)} %reshape.443), calls=%async_computation.1 | async-start | bytes 2621440 | tf_op jit(solution)/shard_map/all_to_all | solution.py:189
  171.2 77.8 %all-gather.20.cloned.1.call-start = ((), (), s32[]{:S(2)}) async-start(), calls=%async_computation.19 | async-start | bytes 2949120 | tf_op jit(solution)/shard_map/all_gather | solution.py:142
  276.8 36.5 %all-to-all-start.2 = ((bf16[640,4,256]{2,0,1:T(8,128)(2,1)}), bf16[640,4,256]{2,0,1:T(8,128)(2,1)}, u32[]{:S(2)}, u32[]{:S(2)}) async-start(bf16[640,4,256]{2,0,1:T(8,128)(2,1)} %bitcast.176), calls=%async_computation.2 | async-start | bytes 2621440 | tf_op jit(solution)/shard_map/all_to_all | solution.py:245
  281.4 203.7 %reduce-scatter.28.cloned.1.call-start = ((), (), s32[]{:S(2)}) async-start(), calls=%async_computation.28 | async-start | bytes 1638400
  455.6 61.9 %reduce-scatter.12.cloned.1.call-start = ((), (), s32[]{:S(2)}) async-start(), calls=%async_computation.20 | async-start | bytes 1638400 | tf_op jit(solution)/shard_map/reduce_scatter | solution.py:256
  456.9 30.9 %copy-start.12 = (f32[640,256]{0,1:T(8,128)S(1)}, f32[640,256]{0,1:T(8,128)}, u32[]{:S(2)}) copy-start(f32[640,256]{0,1:T(8,128)} %copy-done.11) | copy-start | bytes 1966084
  456.9 30.9 %copy-start.41 = (f32[640]{0:T(1024)S(1)}, f32[640]{0:T(1024)}, u32[]{:S(2)}) copy-start(f32[640]{0:T(1024)} %copy-done.40) | copy-start | bytes 7684
  456.9 169.7 %reduce-scatter.16.cloned.1.call-start = ((), (), s32[]{:S(2)}) async-start(), calls=%async_computation.22 | async-start | bytes 737280 | tf_op jit(solution)/shard_map/reduce_scatter | solution.py:287
  490.3 137.8 %reduce-scatter.18.cloned.1.call-start = ((), (), s32[]{:S(2)}) async-start(), calls=%async_computation.23 | async-start | bytes 737280 | tf_op jit(solution)/shard_map/reduce_scatter | solution.py:288
  519.8 119.8 %reduce-scatter.20.cloned.1.call-start = ((), (), s32[]{:S(2)}) async-start(), calls=%async_computation.24 | async-start | bytes 2949120 | tf_op jit(solution)/shard_map/reduce_scatter | solution.py:289
  522.7 163.9 %reduce-scatter.14.cloned.1.call-start = ((), (), s32[]{:S(2)}) async-start(), calls=%async_computation.21 | async-start | bytes 2949120 | tf_op jit(solution)/shard_map/reduce_scatter | solution.py:286
  572.4 174.1 %reduce-scatter.22.cloned.1.call-start = ((), (), s32[]{:S(2)}) async-start(), calls=%async_computation.25 | async-start | bytes 5898240 | tf_op jit(solution)/shard_map/reduce_scatter | solution.py:290
  579.8 226.9 %reduce-scatter.24.cloned.1.call-start = ((), (), s32[]{:S(2)}) async-start(), calls=%async_computation.26 | async-start | bytes 5898240 | tf_op jit(solution)/shard_map/reduce_scatter | solution.py:291
  586.2 280.3 %reduce-scatter.26.cloned.1.call-start = ((), (), s32[]{:S(2)}) async-start(), calls=%async_computation.27 | async-start | bytes 5898240 | tf_op jit(solution)/shard_map/reduce_scatter | solution.py:292
  594.0 311.3 %all-reduce.23.cloned.1.call-start = ((), (), s32[]{:S(2)}) async-start(), calls=%async_computation.29 | async-start | bytes 169984 | tf_op jit(solution)/shard_map/psum | solution.py:302
  629.7 341.7 %all-reduce.25.cloned.1.call-start = ((), (), s32[]{:S(2)}) async-start(), calls=%async_computation.30 | async-start | bytes 2621440 | tf_op jit(solution)/shard_map/psum | solution.py:301
  748.3 120.1 %copy-start.15 = (bf16[640,640]{0,1:T(8,128)(2,1)S(1)}, bf16[640,640]{0,1:T(8,128)(2,1)}, u32[]{:S(2)}) copy-start(bf16[640,640]{0,1:T(8,128)(2,1)} %get-tuple-element.454) | copy-start | bytes 2457604
  (97 other events, 513.2 us)
Sparse Core Ops, SparseCore 0:
  10.0 28.3 all-gather.7
  43.4 32.5 all-gather.9
  78.2 49.3 all-gather.11
  129.3 23.8 all-gather.13
  154.9 30.1 all-gather.15
  186.8 30.1 all-gather.17
  218.9 30.1 all-gather.19
  455.7 29.3 reduce-scatter.27
  487.4 30.0 reduce-scatter.11
  521.0 33.3 reduce-scatter.15
  558.1 34.5 reduce-scatter.17
  595.9 43.6 reduce-scatter.19
  643.0 43.6 reduce-scatter.13
  689.9 56.5 reduce-scatter.21
  750.1 56.5 reduce-scatter.23
  809.9 56.5 reduce-scatter.25
  870.7 34.6 all-reduce.22
  909.1 62.2 all-reduce.24
where the time goes:
time: 996 us; the launch traced here: 985 us
  waiting for transfers between devices  505 us (51%)
  matrix products  203 us (20%)
  blocking collectives  92.3 us (9%)
  local copies, waits for them, and re-layouts  76 us (8%)
  other arithmetic  59.7 us (6%)
  between operations  18.2 us (2%)
  loops' own time  17.1 us (2%)
  starting transfers between devices  13.8 us (1%)
    reduce_scatter x1, waiting for transfers between devices, per_device(): lax.psum_scatter(grad_up_weight, 'fsdp', scatter_dimension=0, tiled=True)  58.3 us
    reduce_scatter x1, waiting for transfers between devices, per_device(): lax.psum_scatter(grad_gate_weight, 'fsdp', scatter_dimension=0, tiled=True)  58.2 us
    reduce_scatter x1, waiting for transfers between devices, per_device(): lax.psum_scatter(grad_down_weight, 'fsdp', scatter_dimension=0, tiled=True)  58 us
    psum x1, waiting for transfers between devices, per_device(): lax.psum(scattered[0].astype(jnp.bfloat16), 'seq').astype(jnp.float32)  56.3 us
    all_gather x1, waiting for transfers between devices, per_device(): lax.all_gather(value_low, 'seq', axis=0, tiled=True)  49.1 us
    reduce_scatter x1, waiting for transfers between devices, per_device(): lax.psum_scatter(grad_query_weight, 'fsdp', scatter_dimension=0, tiled=True)  45.4 us
    unnamed x170, local copies, waits for them, and re-layouts  42.3 us
    unnamed x2, blocking collectives  39.2 us
  transfers between devices with their start and end apart: 21, of which 15 were waited for; matrix products, arithmetic and copies ran while one was open for 17% of the time, Pallas kernels for 0%

commit v1 on v0

v1 whole, which is shorter than its diff:
```python
import functools
import math

import jax
import jax.numpy as jnp
from jax import lax
from jax.experimental import pallas as pl
from jax.experimental.pallas import tpu as pltpu
from jax.sharding import PartitionSpec as P

epsilon = 1e-06
rope_base = 1000000.0


def rms_scale(values, gain_row):
    return values * lax.rsqrt(jnp.mean(values * values, -1, keepdims=True) + epsilon) * gain_row


def rotate(values, cosine_table, sine_table):
    half_width = values.shape[-1] // 2
    first_half = values[..., :half_width]
    second = values[..., half_width:]
    return jnp.concatenate(
        [
            first_half * cosine_table - second * sine_table,
            second * cosine_table + first_half * sine_table,
        ],
        -1,
    )


def angles_for(positions, width):
    half_width = width // 2
    frequency = rope_base ** (-(jnp.arange(half_width).astype(jnp.float32) * 2.0 / width))
    angles = positions[:, None] * frequency[None, :]
    return (jnp.cos(angles), jnp.sin(angles))


def gelu_product(gate_lin, up_lin):
    return jax.nn.gelu(gate_lin, approximate=True) * up_lin


def bit_count(axis):
    return lax.axis_size(axis).bit_length() - 1


def my_bit(axis, bit):
    return (lax.axis_index(axis) >> bit) & 1


def flip_pairs(axis, bit):
    return [(i, i ^ (1 << bit)) for i in range(lax.axis_size(axis))]


def gather_order(axis, forward):
    upper = list(range(1, bit_count(axis)))
    return (upper if forward else upper[::-1]) + [0]


def gather_rows(block, forward):
    axis = "fsdp"
    bits = bit_count(axis)
    grid_shape = (2,) * bits
    buffer = jnp.zeros(grid_shape + block.shape, block.dtype)
    tail = (0,) * block.ndim
    own = [my_bit(axis, bits - 1 - d) for d in range(bits)]
    buffer = lax.dynamic_update_slice(
        buffer, block.reshape((1,) * bits + block.shape), tuple(own) + tail
    )
    piece = block.reshape((1,) * bits + block.shape)
    done = set()
    for step, bit in enumerate(gather_order(axis, forward)):
        if step:
            starts = [0 if bits - 1 - d in done else own[d] for d in range(bits)]
            sizes = tuple(2 if bits - 1 - d in done else 1 for d in range(bits))
            piece = lax.dynamic_slice(buffer, tuple(starts) + tail, sizes + block.shape)
        arrived = lax.ppermute(piece, axis, flip_pairs(axis, bit))
        starts = [0 if bits - 1 - d in done else own[d] for d in range(bits)]
        starts[bits - 1 - bit] = 1 - own[bits - 1 - bit]
        buffer = lax.dynamic_update_slice(buffer, arrived, tuple(starts) + tail)
        done.add(bit)
    return buffer.reshape((-1,) + block.shape)


def scatter_rows(values, forward):
    axis = "fsdp"
    bits = bit_count(axis)
    block_shape = values.shape[1:]
    buffer = values.astype(jnp.bfloat16).reshape((2,) * bits + block_shape)
    for bit in gather_order(axis, forward)[::-1]:
        dim = bits - 1 - bit
        mine = my_bit(axis, bit)
        kept = lax.dynamic_slice_in_dim(buffer, mine, 1, dim)
        sent = lax.dynamic_slice_in_dim(buffer, 1 - mine, 1, dim)
        arrived = lax.ppermute(sent, axis, flip_pairs(axis, bit))
        total = kept.astype(jnp.float32) + arrived.astype(jnp.float32)
        buffer = total.astype(jnp.bfloat16)
    return buffer.reshape(block_shape)


def seq_sum(shard):
    axis = "seq"
    count = lax.axis_size(axis)
    me = lax.axis_index(axis)
    dim = 1 if shard.shape[1] % (128 * count) == 0 else 0
    width = shard.shape[dim] // count
    total = lax.dynamic_slice_in_dim(shard, me * width, width, dim).astype(jnp.float32)
    for shift in range(1, count):
        to = (me + shift) % count
        sent = lax.dynamic_slice_in_dim(shard, to * width, width, dim)
        pairs = [(i, (i + shift) % count) for i in range(count)]
        total = total + lax.ppermute(sent, axis, pairs).astype(jnp.float32)
    part = total.astype(jnp.bfloat16)
    result = lax.dynamic_update_slice_in_dim(jnp.zeros_like(shard), part, me * width, dim)
    for shift in range(1, count):
        pairs = [(i, (i + shift) % count) for i in range(count)]
        arrived = lax.ppermute(part, axis, pairs)
        result = lax.dynamic_update_slice_in_dim(
            result, arrived, ((me - shift + count) % count) * width, dim
        )
    return result


def dims(left, right):
    return (((left,), (right,)), ((), ()))


def f32_dot(left, right, left_dim, right_dim):
    return lax.dot_general(
        left, right, dims(left_dim, right_dim), preferred_element_type=jnp.float32
    )


def forward_kernel(slots, key_tile, factor, place_ref, query_ref, *refs):
    kv_refs = refs[:slots]
    out_ref, total_ref, sum_ref, acc_ref = refs[slots:]
    rows, width = query_ref.shape
    sum_ref[...] = jnp.zeros_like(sum_ref)
    acc_ref[...] = jnp.zeros_like(acc_ref)

    def tile(kv_ref, start, masked):
        keys = kv_ref[pl.ds(start, key_tile), :width]
        values = kv_ref[pl.ds(start, key_tile), width:]
        weights = jnp.exp2(f32_dot(keys, query_ref[...], 1, 1) * factor)
        if masked:
            key_pos = start + lax.broadcasted_iota(jnp.int32, weights.shape, 0)
            query_pos = lax.broadcasted_iota(jnp.int32, weights.shape, 1)
            weights = jnp.where(key_pos <= query_pos, weights, 0.0)
        sum_ref[...] += jnp.sum(weights, 0, keepdims=True)
        acc_ref[...] += f32_dot(values, weights.astype(jnp.bfloat16), 0, 0)

    for slot in range(slots):

        @pl.when(slot <= place_ref[0])
        def _(slot=slot):
            for start in range(0, rows, key_tile):
                tile(kv_refs[slot], start, slot == 0)

    total = sum_ref[...]
    total_ref[...] = total[None]
    out_ref[...] = (acc_ref[...] / total).T.astype(out_ref.dtype)


def attend_forward(place, query, kv_list, heads):
    rows = query.shape[0]
    width = query.shape[1] // heads
    slots = len(kv_list)
    kernel = functools.partial(
        forward_kernel, slots, rows // 2, math.log2(math.e) * width**-0.5
    )
    return pl.pallas_call(
        kernel,
        grid_spec=pltpu.PrefetchScalarGridSpec(
            num_scalar_prefetch=1,
            grid=(heads,),
            in_specs=[pl.BlockSpec((rows, width), lambda h, p: (0, h))]
            + [pl.BlockSpec((rows, 2 * width), lambda h, p: (0, 0))] * slots,
            out_specs=[
                pl.BlockSpec((rows, width), lambda h, p: (0, h)),
                pl.BlockSpec((1, 1, rows), lambda h, p: (h, 0, 0)),
            ],
            scratch_shapes=[
                pltpu.VMEM((1, rows), jnp.float32),
                pltpu.VMEM((width, rows), jnp.float32),
            ],
        ),
        out_shape=[
            jax.ShapeDtypeStruct(query.shape, jnp.bfloat16),
            jax.ShapeDtypeStruct((heads, 1, rows), jnp.float32),
        ],
        compiler_params=pltpu.CompilerParams(vmem_limit_bytes=40 * 2**20),
        cost_estimate=pl.CostEstimate(
            flops=4 * slots * heads * rows * rows * width,
            bytes_accessed=8 * rows * width * heads,
            transcendentals=slots * heads * rows * rows,
        ),
    )(place, query, *kv_list)


def backward_kernel(slots, key_tile, factor, scale, place_ref, query_ref, grad_ref, *refs):
    log_ref, delta_ref = refs[:2]
    kv_refs = refs[2 : 2 + slots]
    query_grad_ref = refs[2 + slots]
    kv_grad_refs = refs[3 + slots : 3 + 2 * slots]
    acc_ref, total_ref = refs[3 + 2 * slots :]
    rows, width = query_ref.shape
    head = pl.program_id(0)

    @pl.when(head == 0)
    def _():
        total_ref[...] = jnp.zeros_like(total_ref)

    acc_ref[...] = jnp.zeros_like(acc_ref)

    def tile(slot, start, masked):
        kv_ref = kv_refs[slot]
        here = pl.ds(start, key_tile)
        keys = kv_ref[here, :width]
        values = kv_ref[here, width:]
        weights = jnp.exp2(f32_dot(keys, query_ref[...], 1, 1) * factor - log_ref[0])
        if masked:
            key_pos = start + lax.broadcasted_iota(jnp.int32, weights.shape, 0)
            query_pos = lax.broadcasted_iota(jnp.int32, weights.shape, 1)
            weights = jnp.where(key_pos <= query_pos, weights, 0.0)
        grad_weights = f32_dot(values, grad_ref[...], 1, 1)
        grad_scores = (weights * (grad_weights - delta_ref[0])).astype(jnp.bfloat16)
        total_ref[slot, here, width:] += f32_dot(
            weights.astype(jnp.bfloat16), grad_ref[...], 1, 0
        )
        total_ref[slot, here, :width] += f32_dot(grad_scores, query_ref[...], 1, 0)
        acc_ref[...] += f32_dot(grad_scores, keys, 0, 0)

    for slot in range(slots):

        @pl.when(slot <= place_ref[0])
        def _(slot=slot):
            for start in range(0, rows, key_tile):
                tile(slot, start, slot == 0)

    query_grad_ref[...] = (acc_ref[...] * scale).astype(query_grad_ref.dtype)

    @pl.when(head == pl.num_programs(0) - 1)
    def _():
        for slot in range(slots):
            kv_grad_refs[slot][:, :width] = (total_ref[slot, :, :width] * scale).astype(
                jnp.bfloat16
            )
            kv_grad_refs[slot][:, width:] = total_ref[slot, :, width:].astype(jnp.bfloat16)


def attend_backward(place, query, grad_rows, log_totals, delta, kv_list, heads):
    rows = query.shape[0]
    width = query.shape[1] // heads
    slots = len(kv_list)
    scale = width**-0.5
    kernel = functools.partial(
        backward_kernel, slots, rows // 2, math.log2(math.e) * scale, scale
    )
    head_spec = pl.BlockSpec((rows, width), lambda h, p: (0, h))
    line_spec = pl.BlockSpec((1, 1, rows), lambda h, p: (h, 0, 0))
    kv_spec = pl.BlockSpec((rows, 2 * width), lambda h, p: (0, 0))
    return pl.pallas_call(
        kernel,
        grid_spec=pltpu.PrefetchScalarGridSpec(
            num_scalar_prefetch=1,
            grid=(heads,),
            in_specs=[head_spec, head_spec, line_spec, line_spec] + [kv_spec] * slots,
            out_specs=[head_spec] + [kv_spec] * slots,
            scratch_shapes=[
                pltpu.VMEM((rows, width), jnp.float32),
                pltpu.VMEM((slots, rows, 2 * width), jnp.float32),
            ],
        ),
        out_shape=[jax.ShapeDtypeStruct(query.shape, jnp.bfloat16)]
        + [jax.ShapeDtypeStruct((rows, 2 * width), jnp.bfloat16)] * slots,
        compiler_params=pltpu.CompilerParams(vmem_limit_bytes=48 * 2**20),
        cost_estimate=pl.CostEstimate(
            flops=10 * slots * heads * rows * rows * width,
            bytes_accessed=12 * rows * width * heads,
            transcendentals=slots * heads * rows * rows,
        ),
    )(place, query, grad_rows, log_totals, delta, *kv_list)


def up_pairs(shift):
    return [(i, i + shift) for i in range(lax.axis_size("seq") - shift)]


def down_pairs(shift):
    return [(i + shift, i) for i in range(lax.axis_size("seq") - shift)]


def mm(left, right):
    return jnp.dot(left, right, preferred_element_type=jnp.float32)


def mm_nt(left, right):
    return f32_dot(left, right, 1, 1)


def mm_tn(left, right):
    return f32_dot(left, right, 0, 0)


def per_device(
    block_in,
    query_weight,
    key_weight,
    value_weight,
    output_weight,
    gate_weight,
    up_weight,
    down_weight,
    attention_norm,
    query_norm,
    key_norm,
    post_attention_norm,
    feedforward_norm,
    post_feedforward_norm,
    grad_out,
):
    parts = lax.axis_size("fsdp")
    gains = (
        attention_norm,
        query_norm,
        key_norm,
        post_attention_norm,
        feedforward_norm,
        post_feedforward_norm,
    )
    gain_sizes = [g.shape[0] for g in gains]
    gain_total = sum(gain_sizes)
    kv_rows, kv_width = key_weight.shape[0], 2 * key_weight.shape[1]
    kv_block = jnp.concatenate([key_weight, value_weight], 1)
    extra_rows = 16
    gain_block = jnp.concatenate(
        gains + (jnp.zeros((extra_rows * kv_width - gain_total,), jnp.bfloat16),)
    ).reshape(extra_rows, kv_width)
    kv_gathered = gather_rows(jnp.concatenate([kv_block, gain_block], 0), False)
    query_full = gather_rows(query_weight, True).reshape(-1, query_weight.shape[1])
    kv_full = kv_gathered[:, :kv_rows].reshape(-1, kv_width)
    gain_rows = kv_gathered[:, kv_rows:].reshape(parts, -1).astype(jnp.float32)
    split_gains = []
    offset = 0
    for size in gain_sizes:
        split_gains.append(gain_rows[:, offset : offset + size].reshape(-1))
        offset += size
    attention_gain, query_gain, key_gain, post_attention_gain, second_gain, post_second_gain = (
        split_gains
    )
    output_full = gather_rows(output_weight, True).reshape(-1, output_weight.shape[1])
    up_full = gather_rows(up_weight, False).reshape(-1, up_weight.shape[1])
    gate_full = gather_rows(gate_weight, True).reshape(-1, gate_weight.shape[1])
    down_full = gather_rows(down_weight, False).reshape(-1, down_weight.shape[1])

    token_count = block_in.shape[0]
    head_size = query_gain.shape[0]
    head_count = query_full.shape[1] // head_size
    slots = lax.axis_size("seq")
    seq_place = lax.axis_index("seq")
    place = seq_place.astype(jnp.int32).reshape(1)
    input_f = block_in.astype(jnp.float32)
    normed, pull_normed = jax.vjp(rms_scale, input_f, attention_gain)
    normed_low = normed.astype(jnp.bfloat16)
    kv_lin = mm(normed_low, kv_full)
    key_lin = kv_lin[:, :head_size]
    value_low = kv_lin[:, head_size:].astype(jnp.bfloat16)
    positions = (seq_place * token_count + jnp.arange(token_count, dtype=jnp.int32)).astype(
        jnp.float32
    )
    cosine_table, sine_table = angles_for(positions, head_size)

    def query_piece(values, gain_row):
        return rotate(rms_scale(values, gain_row), cosine_table[:, None, :], sine_table[:, None, :])

    def key_piece(values, gain_row):
        return rotate(rms_scale(values, gain_row), cosine_table, sine_table)

    key_rows, pull_keys = jax.vjp(key_piece, key_lin, key_gain)
    kv_own = jnp.concatenate([key_rows.astype(jnp.bfloat16), value_low], 1)
    kv_list = [kv_own] + [lax.ppermute(kv_own, "seq", up_pairs(s)) for s in range(1, slots)]
    query_lin = mm(normed_low, query_full).reshape(token_count, head_count, head_size)
    queries, pull_queries = jax.vjp(query_piece, query_lin, query_gain)
    queries_low = queries.astype(jnp.bfloat16).reshape(token_count, head_count * head_size)
    mixed, totals = attend_forward(place, queries_low, kv_list, head_count)
    attended = mm(mixed, output_full)
    post_branch, pull_post = jax.vjp(rms_scale, attended, post_attention_gain)
    residual = input_f + post_branch
    normed_second, pull_second = jax.vjp(rms_scale, residual, second_gain)
    second_low = normed_second.astype(jnp.bfloat16)
    gate_lin = mm(second_low, gate_full)
    up_lin = mm(second_low, up_full)
    activated, pull_activated = jax.vjp(gelu_product, gate_lin, up_lin)
    activated_low = activated.astype(jnp.bfloat16)
    down_lin = mm(activated_low, down_full)
    tail_branch, pull_tail = jax.vjp(rms_scale, down_lin, post_second_gain)
    block_out = (residual + tail_branch).astype(jnp.bfloat16)
    grad_f = grad_out.astype(jnp.float32)
    grad_down, grad_post_second = pull_tail(grad_f)
    grad_down_low = grad_down.astype(jnp.bfloat16)

    def reduced(left, right, forward):
        product = mm_tn(left, right).astype(jnp.bfloat16)
        return scatter_rows(product.reshape(parts, -1, product.shape[1]), forward)

    sum_down = reduced(activated_low, grad_down_low, False)
    grad_activated = mm_nt(grad_down_low, down_full)
    grad_gate, grad_up = pull_activated(grad_activated)
    gate_low = grad_gate.astype(jnp.bfloat16)
    up_low = grad_up.astype(jnp.bfloat16)
    sum_gate = reduced(second_low, gate_low, True)
    sum_up = reduced(second_low, up_low, False)
    grad_second = mm_nt(gate_low, gate_full) + mm_nt(up_low, up_full)
    grad_resid_part, grad_second_gain = pull_second(grad_second)
    grad_residual = grad_f + grad_resid_part
    grad_attended, grad_post_attention = pull_post(grad_residual)
    attended_low = grad_attended.astype(jnp.bfloat16)
    sum_output = reduced(mixed, attended_low, True)
    grad_mixed = mm_nt(attended_low, output_full).astype(jnp.bfloat16)
    delta = jnp.sum(
        (grad_mixed.astype(jnp.float32) * mixed.astype(jnp.float32)).reshape(
            token_count, head_count, head_size
        ),
        -1,
    ).T.reshape(head_count, 1, token_count)
    outs = attend_backward(
        place, queries_low, grad_mixed, jnp.log2(totals), delta, kv_list, head_count
    )
    grad_queries, kv_grads = outs[0], outs[1:]
    kv_grad = kv_grads[0].astype(jnp.float32)
    for shift in range(1, slots):
        arrived = lax.ppermute(kv_grads[shift], "seq", down_pairs(shift))
        kv_grad = kv_grad + arrived.astype(jnp.float32)
    kv_grad = kv_grad.astype(jnp.bfloat16)
    grad_query_lin, grad_query_gain = pull_queries(
        grad_queries.astype(jnp.float32).reshape(query_lin.shape)
    )
    query_lin_low = grad_query_lin.reshape(token_count, head_count * head_size).astype(jnp.bfloat16)
    sum_query = reduced(normed_low, query_lin_low, True)
    grad_normed = mm_nt(query_lin_low, query_full)
    grad_key_lin, grad_key_gain = pull_keys(kv_grad[:, :head_size].astype(jnp.float32))
    kv_lin_low = jnp.concatenate(
        [grad_key_lin.astype(jnp.bfloat16), kv_grad[:, head_size:]], 1
    )
    grad_normed = grad_normed + mm_nt(kv_lin_low, kv_full)
    grad_input_part, grad_attention_gain = pull_normed(grad_normed)
    grad_in = (grad_residual + grad_input_part).astype(jnp.bfloat16)
    gain_grads = (
        grad_attention_gain,
        grad_query_gain,
        grad_key_gain,
        grad_post_attention,
        grad_second_gain,
        grad_post_second,
    )
    gain_grad_rows = jnp.concatenate(
        [g.astype(jnp.bfloat16).reshape(parts, -1) for g in gain_grads]
        + [jnp.zeros((parts, extra_rows * kv_width - gain_total), jnp.bfloat16)],
        1,
    ).reshape(parts, extra_rows, kv_width)
    kv_product = mm_tn(normed_low, kv_lin_low).astype(jnp.bfloat16).reshape(
        parts, kv_rows, kv_width
    )
    sum_kv = scatter_rows(jnp.concatenate([kv_product, gain_grad_rows], 1), False)

    down_sum = seq_sum(sum_down).astype(jnp.float32)
    gate_sum = seq_sum(sum_gate).astype(jnp.float32)
    up_sum = seq_sum(sum_up).astype(jnp.float32)
    output_sum = seq_sum(sum_output).astype(jnp.float32)
    query_sum = seq_sum(sum_query).astype(jnp.float32)
    kv_sum = seq_sum(sum_kv).astype(jnp.float32)
    gain_sum = kv_sum[kv_rows:].reshape(-1)
    gain_outs = []
    offset = 0
    for size in gain_sizes:
        gain_outs.append(gain_sum[offset : offset + size])
        offset += size
    return (
        block_out,
        grad_in,
        query_sum,
        kv_sum[:kv_rows, :head_size],
        kv_sum[:kv_rows, head_size:],
        output_sum,
        gate_sum,
        up_sum,
        down_sum,
        *gain_outs,
    )


def solution(mesh):
    in_specs = (
        P(("fsdp", "seq"), None),
        P("fsdp", None),
        P("fsdp", None),
        P("fsdp", None),
        P("fsdp", None),
        P("fsdp", None),
        P("fsdp", None),
        P("fsdp", None),
        P("fsdp"),
        P("fsdp"),
        P("fsdp"),
        P("fsdp"),
        P("fsdp"),
        P("fsdp"),
        P(("fsdp", "seq"), None),
    )
    out_specs = (
        P(("fsdp", "seq"), None),
        P(("fsdp", "seq"), None),
        P("fsdp", None),
        P("fsdp", None),
        P("fsdp", None),
        P("fsdp", None),
        P("fsdp", None),
        P("fsdp", None),
        P("fsdp", None),
        P("fsdp"),
        P("fsdp"),
        P("fsdp"),
        P("fsdp"),
        P("fsdp"),
        P("fsdp"),
    )
    return jax.shard_map(
        per_device, mesh=mesh, in_specs=in_specs, out_specs=out_specs, check_vma=False
    )
```

time: 996 us -> 453 us (0.45)
  waiting for transfers between devices: 505 us -> 134 us
  matrix products: 203 us -> 56 us
  blocking collectives: 92.3 us -> 0 us
  starting transfers between devices: 13.8 us -> 96.9 us
  local copies, waits for them, and re-layouts: 76 us -> 101 us
  other arithmetic: 59.7 us -> 39.2 us
  loops' own time: 17.1 us -> 0 us
  Pallas kernels: 0 us -> 16.4 us
  between operations: 18.2 us -> 2.28 us
    reduce_scatter x8 -> x0, waiting for transfers between devices: 257 us -> none  [the longest x1 58.3 us: per_device(): lax.psum_scatter(grad_up_weight, 'fsdp', scatter_dimension=0, tiled=True)]
    dot_general x56 -> x18, matrix products: 203 us -> 56 us  [the longest x12 37.9 us: f32_dot(): lax.dot_general(left, right, dims(left_dim, right_dim), preferred_element...]
    ppermute x0 -> x78, waiting for transfers between devices: none -> 134 us  [the longest x3 78.6 us: per_device(): arrived = lax.ppermute(kv_grads[shift], 'seq', down_pairs(shift))]
    ppermute x0 -> x78, starting transfers between devices: none -> 96.9 us  [the longest x18 25.6 us: seq_sum(): total = total + lax.ppermute(sent, axis, pairs).astype(jnp.float32)]
    psum x2 -> x0, waiting for transfers between devices: 88.4 us -> none  [the longest x1 56.3 us: per_device(): lax.psum(scattered[0].astype(jnp.bfloat16), 'seq').astype(jnp.float32)]
    all_gather x7 -> x0, waiting for transfers between devices: 67.5 us -> none  [the longest x1 49.1 us: per_device(): lax.all_gather(value_low, 'seq', axis=0, tiled=True)]
    all_to_all x3 -> x0, waiting for transfers between devices: 61.3 us -> none  [the longest x1 31.9 us: per_device(): lax.all_to_all(grad_mixed, 'seq', split_axis=1, concat_axis=0, tiled=True)]
    unnamed x2 -> x0, blocking collectives: 39.2 us -> none
  transfers between devices with their start and end apart: 21 -> 78, of which waited for: 15 -> 27; matrix products, arithmetic and copies ran while one was open for 17% -> 31% of each run, Pallas kernels for 0% -> 4%
where the time goes in v1:
time: 453 us; the launch traced here: 446 us
  waiting for transfers between devices  134 us (30%)
  local copies, waits for them, and re-layouts  101 us (22%)
  starting transfers between devices  96.9 us (21%)
  matrix products  56 us (12%)
  other arithmetic  39.2 us (9%)
  Pallas kernels  16.4 us (4%)
    ppermute x3, waiting for transfers between devices, per_device(): arrived = lax.ppermute(kv_grads[shift], 'seq', down_pairs(shift))  78.6 us
    dot_general x12, matrix products, f32_dot(): lax.dot_general(left, right, dims(left_dim, right_dim), preferred_element...  37.9 us
    ppermute x18, waiting for transfers between devices, seq_sum(): arrived = lax.ppermute(part, axis, pairs)  31.6 us
    ppermute x18, starting transfers between devices, seq_sum(): total = total + lax.ppermute(sent, axis, pairs).astype(jnp.float32)  25.6 us
    dynamic_update_slice x18, local copies, waits for them, and re-layouts, gather_rows(): buffer = lax.dynamic_update_slice(buffer, arrived, tuple(starts) + tail)  24.2 us
    ppermute x18, starting transfers between devices, seq_sum(): arrived = lax.ppermute(part, axis, pairs)  23.5 us
    dynamic_slice x12, local copies, waits for them, and re-layouts, gather_rows(): piece = lax.dynamic_slice(buffer, tuple(starts) + tail, sizes + block.shape)  19.4 us
    dot_general x6, matrix products, mm(): return jnp.dot(left, right, preferred_element_type=jnp.float32)  18.1 us
  transfers between devices with their start and end apart: 78, of which 27 were waited for; matrix products, arithmetic and copies ran while one was open for 31% of the time, Pallas kernels for 4%

profile of v1, /device:TPU:0, one launch (start us, length us, event | category | flops | bytes accessed | tf_op | source)
XLA Modules:
  0.0 445.9 jit_solution(1953964804130531312)
XLA Ops:
  0.7 4.1 concatenate.34
  66.7 4.0 collective-permute-start.6
  72.7 4.5 %collective-permute-start.7 = (bf16[640,512]{1,0:T(8,128)(2,1)S(1)}, bf16[640,512]{1,0:T(8,128)(2,1)S(1)}, u32[]{:S(2)}, u32[]{:S(2)}) collective-permute-start(bf16[640,512]{1,0:T(8,128)(2,1)S(1)} %pad_maximum_fusion.1.refs_0_.refs_2_), channel_id=1, source_target_pairs={{0,2},{1,3},{4,6},{5,7},{8,10},{9,11},{12,14},{13,15},{16,18},{17,... | collective-permute-start | bytes 1966088 | tf_op jit(solution)/shard_map/ppermute | solution.py:381
  79.2 6.3 %collective-permute-start.8 = (bf16[640,512]{1,0:T(8,128)(2,1)S(1)}, bf16[640,512]{1,0:T(8,128)(2,1)}, u32[]{:S(2)}, u32[]{:S(2)}) collective-permute-start(bf16[640,512]{1,0:T(8,128)(2,1)S(1)} %pad_maximum_fusion.1.refs_0_.refs_2_), channel_id=1, source_target_pairs={{0,3},{4,7},{8,11},{12,15},{16,19},{20,23},{24,27},{28,31}} | collective-permute-start | bytes 1966088 | tf_op jit(solution)/shard_map/ppermute | solution.py:381
  109.1 3.8 collective-permute-done.8.refs_3_.refs_5_
  112.9 6.1 %shard_map.262 = (bf16[640,1024]{1,0:T(8,128)(2,1)S(1)}, f32[4,1,640]{2,1,0:T(1,128)S(1)}) custom-call(s32[1]{0:T(128)} %bitcast.place_ref, bf16[640,1024]{1,0:T(8,128)(2,1)S(1)} %copy.89.query_ref, bf16[640,512]{1,0:T(8,128)(2,1)S(1)} %pad_maximum_fusion.1.refs_0_.refs_2_, bf16[640,512]{1,0:T(8,128)(2,1)S(1)} %collective-permute-done.6.refs_1_.refs_3_, ...), custom_call_target="tpu_custom_call" | custom-call | flops 6710886400 | bytes 5242880 | tf_op jit(solution)/shard_map/pallas_call | solution.py:171
  128.5 5.4 %multiply_convert_fusion.1 = (bf16[640,2048]{1,0:T(8,128)(2,1)S(1)}, f32[640,2048]{1,0:T(8,128)S(1)}) fusion(f32[640,2048]{1,0:T(8,128)S(1)} %fusion.88, bf16[640,640]{0,1:T(8,128)(2,1)S(1)} %multiply_convert_fusion.2, bf16[640,2048]{1,0:T(8,128)(2,1)} %bitcast.15), kind=kOutput, calls=%fused_computation.10 | convolution fusion | flops 1690828800 | bytes 16547840 | tf_op jit(solution)/shard_map/dot_general | solution.py:294
  135.1 4.1 multiply_reduce_fusion.7
  144.4 8.4 %fusion.6 = (bf16[640,2048]{1,0:T(8,128)(2,1)S(1)}, bf16[640,2048]{1,0:T(8,128)(2,1)S(1)}) fusion(f32[640,2048]{1,0:T(8,128)S(1)} %fusion.88, f32[640,2048]{1,0:T(8,128)S(1)} %get-tuple-element.154, bf16[640,640]{0,1:T(8,128)(2,1)S(1)} %get-tuple-element.107, bf16[2048,640]{1,0:T(8,128)(2,1)} %bitcast.17), kind=kOutput, calls=%fused_computation.8 | convolution fusion | flops 1709178880 | bytes 19169280 | tf_op jit(solution)/shard_map/dot_general | solution.py:129
  152.7 3.7 convolution_convert_fusion.1
  156.5 4.0 fusion.89
  170.2 5.0 %convert_multiply_fusion.4 = (f32[640,1024]{1,0:T(8,128)}, bf16[640,1024]{1,0:T(8,128)(2,1)}) fusion(bf16[640,1024]{1,0:T(8,128)(2,1)S(1)} %get-tuple-element.22, bf16[640,640]{0,1:T(8,128)(2,1)S(1)} %fusion.17, bf16[1024,640]{1,0:T(8,128)(2,1)} %bitcast.11), kind=kOutput, calls=%fused_computation.28 | convolution fusion | flops 841482240 | bytes 7372800 | tf_op jit(solution)/shard_map/dot_general | solution.py:129
  177.8 4.4 reshape.348
  184.9 10.3 %shard_map.263 = (bf16[640,1024]{1,0:T(8,128)(2,1)}, bf16[640,512]{1,0:T(8,128)(2,1)S(1)}, bf16[640,512]{1,0:T(8,128)(2,1)S(1)}, bf16[640,512]{1,0:T(8,128)(2,1)S(1)}, bf16[640,512]{1,0:T(8,128)(2,1)S(1)}) custom-call(s32[1]{0:T(128)} %bitcast.place_ref, bf16[640,1024]{1,0:T(8,128)(2,1)} %copy-done, bf16[640,1024]{1,0:T(8,128)(2,1)} %get-tuple-element.159.grad_ref, ...), custom_call_target="tpu_custom_call" | custom-call | flops 16777216000 | bytes 7864320 | tf_op jit(solution)/shard_map/pallas_call | solution.py:262
  220.3 28.0 %collective-permute-done.21 = bf16[640,512]{1,0:T(8,128)(2,1)} collective-permute-done((bf16[640,512]{1,0:T(8,128)(2,1)S(1)}, bf16[640,512]{1,0:T(8,128)(2,1)}, u32[]{:S(2)}, u32[]{:S(2)}) %collective-permute-start.21) | collective-permute-done | bytes 655392 | tf_op jit(solution)/shard_map/ppermute | solution.py:432
  248.3 15.2 %collective-permute-done.22 = bf16[640,512]{1,0:T(8,128)(2,1)} collective-permute-done((bf16[640,512]{1,0:T(8,128)(2,1)S(1)}, bf16[640,512]{1,0:T(8,128)(2,1)}, u32[]{:S(2)}, u32[]{:S(2)}) %collective-permute-start.22) | collective-permute-done | bytes 655392 | tf_op jit(solution)/shard_map/ppermute | solution.py:432
  265.0 35.4 %collective-permute-done.23 = bf16[640,512]{1,0:T(8,128)(2,1)} collective-permute-done((bf16[640,512]{1,0:T(8,128)(2,1)S(1)}, bf16[640,512]{1,0:T(8,128)(2,1)}, u32[]{:S(2)}, u32[]{:S(2)}) %collective-permute-start.23) | collective-permute-done | bytes 655392 | tf_op jit(solution)/shard_map/ppermute | solution.py:432
  306.3 3.9 fusion.13
  320.6 4.1 collective-permute-done.25
  342.9 3.8 collective-permute-done.48
  346.7 5.2 %collective-permute-done.49 = bf16[32,640]{1,0:T(8,128)(2,1)S(1)} collective-permute-done((bf16[32,640]{1,0:T(8,128)(2,1)S(1)}, bf16[32,640]{1,0:T(8,128)(2,1)S(1)}, u32[]{:S(2)}, u32[]{:S(2)}) %collective-permute-start.49) | collective-permute-done | bytes 40992 | tf_op jit(solution)/shard_map/ppermute | solution.py:117
  356.0 5.8 %collective-permute-done.30 = bf16[80,256]{1,0:T(8,128)(2,1)S(1)} collective-permute-done((bf16[80,256]{1,0:T(8,128)(2,1)S(1)}, bf16[80,256]{1,0:T(8,128)(2,1)S(1)}, u32[]{:S(2)}, u32[]{:S(2)}) %collective-permute-start.30) | collective-permute-done | bytes 40992 | tf_op jit(solution)/shard_map/ppermute | solution.py:117
  361.8 4.9 %collective-permute-done.31 = bf16[80,256]{1,0:T(8,128)(2,1)S(1)} collective-permute-done((bf16[80,256]{1,0:T(8,128)(2,1)S(1)}, bf16[80,256]{1,0:T(8,128)(2,1)S(1)}, u32[]{:S(2)}, u32[]{:S(2)}) %collective-permute-start.31) | collective-permute-done | bytes 40992 | tf_op jit(solution)/shard_map/ppermute | solution.py:117
  417.4 4.5 %collective-permute-start.55 = (bf16[80,512]{1,0:T(8,128)(2,1)S(1)}, bf16[80,512]{1,0:T(8,128)(2,1)S(1)}, u32[]{:S(2)}, u32[]{:S(2)}) collective-permute-start(bf16[80,512]{1,0:T(8,128)(2,1)S(1)} %get-tuple-element.123), channel_id=1, source_target_pairs={{0,2},{1,3},{2,0},{3,1},{4,6},{5,7},{6,4},{7,5},{8,10},{9,11},{10,... | collective-permute-start | bytes 245768 | tf_op jit(solution)/shard_map/ppermute | solution.py:112
  (463 shorter events, 259.0 us)
Async XLA Ops:
  10.7 24.0 %collective-permute-start.9 = (bf16[1,1,1,128,640]{4,3,2,1,0:T(8,128)(2,1)}, bf16[1,1,1,128,640]{4,3,2,1,0:T(8,128)(2,1)}, u32[]{:S(2)}, u32[]{:S(2)}) collective-permute-start(bf16[1,1,1,128,640]{4,3,2,1,0:T(8,128)(2,1)} %bitcast.171), channel_id=1, source_target_pairs={{0,8},{4,12},{8,0},{12,4},{16,24},{20,28},{24,16},{28,20},{1,9},{5... | collective-permute-start | bytes 491528 | tf_op jit(solution)/shard_map/ppermute | solution.py:77
  11.2 30.0 %collective-permute-start.12 = (bf16[1,1,1,80,2048]{4,3,2,1,0:T(8,128)(2,1)}, bf16[1,1,1,80,2048]{4,3,2,1,0:T(8,128)(2,1)}, u32[]{:S(2)}, u32[]{:S(2)}) collective-permute-start(bf16[1,1,1,80,2048]{4,3,2,1,0:T(8,128)(2,1)} %bitcast.165), channel_id=1, source_target_pairs={{0,8},{4,12},{8,0},{12,4},{16,24},{20,28},{24,16},{28,20},{1,9},{5... | collective-permute-start | bytes 983048 | tf_op jit(solution)/shard_map/ppermute | solution.py:77
  12.7 30.6 %collective-permute-start.15 = (bf16[1,1,1,80,2048]{4,3,2,1,0:T(8,128)(2,1)}, bf16[1,1,1,80,2048]{4,3,2,1,0:T(8,128)(2,1)}, u32[]{:S(2)}, u32[]{:S(2)}) collective-permute-start(bf16[1,1,1,80,2048]{4,3,2,1,0:T(8,128)(2,1)} %bitcast.166), channel_id=1, source_target_pairs={{0,16},{4,20},{8,24},{12,28},{16,0},{20,4},{24,8},{28,12},{1,17},{... | collective-permute-start | bytes 983048 | tf_op jit(solution)/shard_map/ppermute | solution.py:77
  47.2 25.5 %collective-permute-start.16 = (bf16[2,1,1,80,2048]{4,3,2,1,0:T(8,128)(2,1)}, bf16[2,1,1,80,2048]{4,3,2,1,0:T(8,128)(2,1)}, u32[]{:S(2)}, u32[]{:S(2)}) collective-permute-start(bf16[2,1,1,80,2048]{4,3,2,1,0:T(8,128)(2,1)} %constant_dynamic-slice_fusion.24), channel_id=1, source_target_pairs={{0,8},{4,12},{8,0},{12,4},{16,24},{20,28},{24,16},{28,20},{1,9},{5... | collective-permute-start | bytes 1966088 | tf_op jit(solution)/shard_map/ppermute | solution.py:77
  51.9 27.3 %collective-permute-start.19 = (bf16[2,1,1,256,640]{4,3,2,1,0:T(8,128)(2,1)}, bf16[2,1,1,256,640]{4,3,2,1,0:T(8,128)(2,1)}, u32[]{:S(2)}, u32[]{:S(2)}) collective-permute-start(bf16[2,1,1,256,640]{4,3,2,1,0:T(8,128)(2,1)} %constant_dynamic-slice_fusion.22), channel_id=1, source_target_pairs={{0,8},{4,12},{8,0},{12,4},{16,24},{20,28},{24,16},{28,20},{1,9},{5... | collective-permute-start | bytes 1966088 | tf_op jit(solution)/shard_map/ppermute | solution.py:77
  54.7 39.2 %collective-permute-start.5 = (bf16[2,2,1,80,1024]{4,3,2,1,0:T(8,128)(2,1)}, bf16[2,2,1,80,1024]{4,3,2,1,0:T(8,128)(2,1)}, u32[]{:S(2)}, u32[]{:S(2)}) collective-permute-start(bf16[2,2,1,80,1024]{4,3,2,1,0:T(8,128)(2,1)} %constant_dynamic-slice_fusion.29), channel_id=1, source_target_pairs={{0,4},{4,0},{8,12},{12,8},{16,20},{20,16},{24,28},{28,24},{1,5},{5... | collective-permute-start | bytes 1966088 | tf_op jit(solution)/shard_map/ppermute | solution.py:77
  57.4 48.7 %collective-permute-start.11 = (bf16[2,2,1,128,640]{4,3,2,1,0:T(8,128)(2,1)}, bf16[2,2,1,128,640]{4,3,2,1,0:T(8,128)(2,1)}, u32[]{:S(2)}, u32[]{:S(2)}) collective-permute-start(bf16[2,2,1,128,640]{4,3,2,1,0:T(8,128)(2,1)} %constant_dynamic-slice_fusion.27), channel_id=1, source_target_pairs={{0,4},{4,0},{8,12},{12,8},{16,20},{20,16},{24,28},{28,24},{1,5},{5... | collective-permute-start | bytes 1966088 | tf_op jit(solution)/shard_map/ppermute | solution.py:77
  66.7 42.0 %collective-permute-start.6 = (bf16[640,512]{1,0:T(8,128)(2,1)S(1)}, bf16[640,512]{1,0:T(8,128)(2,1)S(1)}, u32[]{:S(2)}, u32[]{:S(2)}) collective-permute-start(bf16[640,512]{1,0:T(8,128)(2,1)S(1)} %pad_maximum_fusion.1.refs_0_.refs_2_), channel_id=1, source_target_pairs={{0,1},{1,2},{2,3},{4,5},{5,6},{6,7},{8,9},{9,10},{10,11},{12,13},{... | collective-permute-start | bytes 1966088 | tf_op jit(solution)/shard_map/ppermute | solution.py:381
  72.7 36.5 %collective-permute-start.7 = (bf16[640,512]{1,0:T(8,128)(2,1)S(1)}, bf16[640,512]{1,0:T(8,128)(2,1)S(1)}, u32[]{:S(2)}, u32[]{:S(2)}) collective-permute-start(bf16[640,512]{1,0:T(8,128)(2,1)S(1)} %pad_maximum_fusion.1.refs_0_.refs_2_), channel_id=1, source_target_pairs={{0,2},{1,3},{4,6},{5,7},{8,10},{9,11},{12,14},{13,15},{16,18},{17,... | collective-permute-start | bytes 1966088 | tf_op jit(solution)/shard_map/ppermute | solution.py:381
  79.2 33.7 %collective-permute-start.8 = (bf16[640,512]{1,0:T(8,128)(2,1)S(1)}, bf16[640,512]{1,0:T(8,128)(2,1)}, u32[]{:S(2)}, u32[]{:S(2)}) collective-permute-start(bf16[640,512]{1,0:T(8,128)(2,1)S(1)} %pad_maximum_fusion.1.refs_0_.refs_2_), channel_id=1, source_target_pairs={{0,3},{4,7},{8,11},{12,15},{16,19},{20,23},{24,27},{28,31}} | collective-permute-start | bytes 1966088 | tf_op jit(solution)/shard_map/ppermute | solution.py:381
  93.9 28.6 %collective-permute-start.14 = (bf16[2,2,1,80,2048]{4,3,2,1,0:T(8,128)(2,1)}, bf16[2,2,1,80,2048]{4,3,2,1,0:T(8,128)(2,1)}, u32[]{:S(2)}, u32[]{:S(2)}) collective-permute-start(bf16[2,2,1,80,2048]{4,3,2,1,0:T(8,128)(2,1)} %constant_dynamic-slice_fusion.25), channel_id=1, source_target_pairs={{0,4},{4,0},{8,12},{12,8},{16,20},{20,16},{24,28},{28,24},{1,5},{5... | collective-permute-start | bytes 3932168 | tf_op jit(solution)/shard_map/ppermute | solution.py:77
  108.7 25.2 %collective-permute-start.20 = (bf16[2,2,1,256,640]{4,3,2,1,0:T(8,128)(2,1)}, bf16[2,2,1,256,640]{4,3,2,1,0:T(8,128)(2,1)S(1)}, u32[]{:S(2)}, u32[]{:S(2)}) collective-permute-start(bf16[2,2,1,256,640]{4,3,2,1,0:T(8,128)(2,1)} %constant_dynamic-slice_fusion.21), channel_id=1, source_target_pairs={{0,4},{4,0},{8,12},{12,8},{16,20},{20,16},{24,28},{28,24},{1,5},{5... | collective-permute-start | bytes 3932168 | tf_op jit(solution)/shard_map/ppermute | solution.py:77
  176.4 196.6 %collective-permute-start.69 = (bf16[2,2,1,256,640]{4,3,2,1,0:T(8,128)(2,1)}, bf16[2,2,1,256,640]{4,3,2,1,0:T(8,128)(2,1)}, u32[]{:S(2)}, u32[]{:S(2)}) collective-permute-start(bf16[2,2,1,256,640]{4,3,2,1,0:T(8,128)(2,1)} %constant_dynamic-slice_fusion.2), channel_id=1, source_target_pairs={{0,4},{4,0},{8,12},{12,8},{16,20},{20,16},{24,28},{28,24},{1,5},{5... | collective-permute-start | bytes 3932168 | tf_op jit(solution)/shard_map/ppermute | solution.py:95
  177.3 40.9 %collective-permute-start.42 = (bf16[2,2,1,128,640]{4,3,2,1,0:T(8,128)(2,1)}, bf16[2,2,1,128,640]{4,3,2,1,0:T(8,128)(2,1)}, u32[]{:S(2)}, u32[]{:S(2)}) collective-permute-start(bf16[2,2,1,128,640]{4,3,2,1,0:T(8,128)(2,1)} %constant_dynamic-slice_fusion.11), channel_id=1, source_target_pairs={{0,4},{4,0},{8,12},{12,8},{16,20},{20,16},{24,28},{28,24},{1,5},{5... | collective-permute-start | bytes 1966088 | tf_op jit(solution)/shard_map/ppermute | solution.py:95
  204.9 43.4 %collective-permute-start.21 = (bf16[640,512]{1,0:T(8,128)(2,1)S(1)}, bf16[640,512]{1,0:T(8,128)(2,1)}, u32[]{:S(2)}, u32[]{:S(2)}) collective-permute-start(bf16[640,512]{1,0:T(8,128)(2,1)S(1)} %copy-done.6), channel_id=1, source_target_pairs={{1,0},{2,1},{3,2},{5,4},{6,5},{7,6},{9,8},{10,9},{11,10},{13,12},{... | collective-permute-start | bytes 1966088 | tf_op jit(solution)/shard_map/ppermute | solution.py:432
  206.2 57.3 %collective-permute-start.22 = (bf16[640,512]{1,0:T(8,128)(2,1)S(1)}, bf16[640,512]{1,0:T(8,128)(2,1)}, u32[]{:S(2)}, u32[]{:S(2)}) collective-permute-start(bf16[640,512]{1,0:T(8,128)(2,1)S(1)} %copy-done.4), channel_id=1, source_target_pairs={{2,0},{3,1},{6,4},{7,5},{10,8},{11,9},{14,12},{15,13},{18,16},{19,... | collective-permute-start | bytes 1966088 | tf_op jit(solution)/shard_map/ppermute | solution.py:432
  207.5 92.9 %collective-permute-start.23 = (bf16[640,512]{1,0:T(8,128)(2,1)S(1)}, bf16[640,512]{1,0:T(8,128)(2,1)}, u32[]{:S(2)}, u32[]{:S(2)}) collective-permute-start(bf16[640,512]{1,0:T(8,128)(2,1)S(1)} %copy-done.2), channel_id=1, source_target_pairs={{3,0},{7,4},{11,8},{15,12},{19,16},{23,20},{27,24},{31,28}} | collective-permute-start | bytes 1966088 | tf_op jit(solution)/shard_map/ppermute | solution.py:432
  218.2 157.9 %collective-permute-start.60 = (bf16[2,2,1,80,2048]{4,3,2,1,0:T(8,128)(2,1)}, bf16[2,2,1,80,2048]{4,3,2,1,0:T(8,128)(2,1)}, u32[]{:S(2)}, u32[]{:S(2)}) collective-permute-start(bf16[2,2,1,80,2048]{4,3,2,1,0:T(8,128)(2,1)} %constant_dynamic-slice_fusion.5), channel_id=1, source_target_pairs={{0,4},{4,0},{8,12},{12,8},{16,20},{20,16},{24,28},{28,24},{1,5},{5... | collective-permute-start | bytes 3932168 | tf_op jit(solution)/shard_map/ppermute | solution.py:95
  248.3 63.7 %collective-permute-start.24 = (bf16[2,2,1,80,1024]{4,3,2,1,0:T(8,128)(2,1)}, bf16[2,2,1,80,1024]{4,3,2,1,0:T(8,128)(2,1)}, u32[]{:S(2)}, u32[]{:S(2)}) collective-permute-start(bf16[2,2,1,80,1024]{4,3,2,1,0:T(8,128)(2,1)} %constant_dynamic-slice_fusion.20), channel_id=1, source_target_pairs={{0,4},{4,0},{8,12},{12,8},{16,20},{20,16},{24,28},{28,24},{1,5},{5... | collective-permute-start | bytes 1966088 | tf_op jit(solution)/shard_map/ppermute | solution.py:95
  263.5 54.3 %collective-permute-start.43 = (bf16[1,2,1,128,640]{4,3,2,1,0:T(8,128)(2,1)}, bf16[1,2,1,128,640]{4,3,2,1,0:T(8,128)(2,1)}, u32[]{:S(2)}, u32[]{:S(2)}) collective-permute-start(bf16[1,2,1,128,640]{4,3,2,1,0:T(8,128)(2,1)} %constant_dynamic-slice_fusion.10), channel_id=1, source_target_pairs={{0,16},{4,20},{8,24},{12,28},{16,0},{20,4},{24,8},{28,12},{1,17},{... | collective-permute-start | bytes 983048 | tf_op jit(solution)/shard_map/ppermute | solution.py:95
  340.3 42.6 %collective-permute-start.51 = (bf16[2,2,1,80,2048]{4,3,2,1,0:T(8,128)(2,1)S(1)}, bf16[2,2,1,80,2048]{4,3,2,1,0:T(8,128)(2,1)S(1)}, u32[]{:S(2)}, u32[]{:S(2)}) collective-permute-start(bf16[2,2,1,80,2048]{4,3,2,1,0:T(8,128)(2,1)S(1)} %copy-done.39), channel_id=1, source_target_pairs={{0,4},{4,0},{8,12},{12,8},{16,20},{20,16},{24,28},{28,24},{1,5},{5... | collective-permute-start | bytes 3932168 | tf_op jit(solution)/shard_map/ppermute | solution.py:95
  340.3 31.1 %collective-permute-start.34 = (bf16[2,1,1,96,512]{4,3,2,1,0:T(8,128)(2,1)S(1)}, bf16[2,1,1,96,512]{4,3,2,1,0:T(8,128)(2,1)S(1)}, u32[]{:S(2)}, u32[]{:S(2)}) collective-permute-start(bf16[2,1,1,96,512]{4,3,2,1,0:T(8,128)(2,1)S(1)} %constant_dynamic-slice_fusion.17), channel_id=1, source_target_pairs={{0,8},{4,12},{8,0},{12,4},{16,24},{20,28},{24,16},{28,20},{1,9},{5... | collective-permute-start | bytes 589832 | tf_op jit(solution)/shard_map/ppermute | solution.py:95
  374.9 23.5 %collective-permute-start.70 = (bf16[2,1,1,256,640]{4,3,2,1,0:T(8,128)(2,1)S(1)}, bf16[2,1,1,256,640]{4,3,2,1,0:T(8,128)(2,1)S(1)}, u32[]{:S(2)}, u32[]{:S(2)}) collective-permute-start(bf16[2,1,1,256,640]{4,3,2,1,0:T(8,128)(2,1)S(1)} %constant_dynamic-slice_fusion.1), channel_id=1, source_target_pairs={{0,8},{4,12},{8,0},{12,4},{16,24},{20,28},{24,16},{28,20},{1,9},{5... | collective-permute-start | bytes 1966088 | tf_op jit(solution)/shard_map/ppermute | solution.py:95
  378.2 23.7 %collective-permute-start.61 = (bf16[2,1,1,80,2048]{4,3,2,1,0:T(8,128)(2,1)S(1)}, bf16[2,1,1,80,2048]{4,3,2,1,0:T(8,128)(2,1)S(1)}, u32[]{:S(2)}, u32[]{:S(2)}) collective-permute-start(bf16[2,1,1,80,2048]{4,3,2,1,0:T(8,128)(2,1)S(1)} %constant_dynamic-slice_fusion.4), channel_id=1, source_target_pairs={{0,8},{4,12},{8,0},{12,4},{16,24},{20,28},{24,16},{28,20},{1,9},{5... | collective-permute-start | bytes 1966088 | tf_op jit(solution)/shard_map/ppermute | solution.py:95
  (109 other events, 1016.6 us)
